TPU v7x, 256 devices: a whole 4x4x8 slice. The times are simulated.
256 devices in a mesh: req: 64 (over x_hi, z, y), own: 4 (over x_lo, core).
Axes of the slice: x: 4 (x_hi: 2, x_lo: 2; x = x_hi * 2 + x_lo), y: 4, z: 8, core: 2. Of those that a mesh axis runs over, the one named last changes fastest.
Arguments:
- tokens: bfloat16 [32768, 16384], P('req', 'own'), may hold values from -600 to 600
- gain: float32 [16384], replicated, may hold values from 0.1 to 1.9
- gate_weight: bfloat16 [16384, 1024], P('req', 'own'), may hold values from -0.046875 to 0.046875
- up_weight: bfloat16 [16384, 1024], P('req', 'own'), may hold values from -0.046875 to 0.046875
- lengths: int32 [256], P('req'), may hold values from 1 to 128, as said below
- dest: int32 [32768], P('req'), may hold values from 0 to 63, as said below
- owner: int32 [4], replicated, may hold values from 0 to 3, each once
Outputs:
- packed_hidden: bfloat16 [16384, 1024], P('req', 'own')
- hidden_rows: bfloat16 [32768, 1024], P('req', 'own')
Inputs may be any that keep to these rules, and one draw needn't show every extreme that they name: `lengths`: each request has 1 to 128 live slots; the live slots of one shard (one index of req) number at most 256, and in every draw some shard has exactly that many. `dest`: counting only live slots, at most 4 slots of one shard name the same shard, and this bound is reached in every draw. Values at slots that are not live are arbitrary.
All inputs are finite; a program needn't handle non-finite values.
Results may differ from a plain program's by a relative error of at most 0.0058.
Values may be sent and summed in bfloat16 or wider, within the bound.
A program may use at most 128 MiB of HBM per device.

v0:
```python
import jax
import jax.numpy as jnp
from jax import lax
from jax.sharding import PartitionSpec as P

norm_eps = 1e-05


def rms_rows(rows, gain):
    wide = rows.astype(jnp.float32)
    scale = lax.rsqrt(jnp.mean(wide * wide, axis=-1, keepdims=True) + norm_eps)
    return (wide * scale * gain).astype(jnp.bfloat16)


def project(normed, gate_weight, up_mine):
    gate_part = jnp.dot(
        normed,
        lax.all_gather(gate_weight, "req", axis=0, tiled=True),
        preferred_element_type=jnp.float32,
    )
    up_part = jnp.dot(
        normed,
        lax.all_gather(up_mine, "req", axis=0, tiled=True),
        preferred_element_type=jnp.float32,
    )
    return (jax.nn.silu(gate_part) * up_part).astype(jnp.bfloat16)


def body(tokens, gain, gate_weight, up_weight, lengths, dest, owner):
    n_req = lax.axis_size("req")
    n_own = lax.axis_size("own")
    tok = tokens.shape[0]
    span = tok // lengths.shape[0]
    hid = gate_weight.shape[1]
    pair = tok // (2 * n_req)
    slots = n_req * pair
    position = jnp.arange(tok, dtype=jnp.int32)
    live = position % span < jnp.repeat(lengths, span)
    marks = ((dest[:, None] == jnp.arange(n_req, dtype=jnp.int32)[None, :]) & live[:, None]).astype(
        jnp.int32
    )
    before = jnp.cumsum(marks, axis=0) - marks
    rank = jnp.sum(before * marks, axis=1)
    place = jnp.where(live, dest * pair + rank, slots)
    source = jnp.zeros((slots,), jnp.int32).at[place].set(position, mode="drop")
    filled = jnp.zeros((slots,), bool).at[place].set(True, mode="drop")
    block_ids = jnp.arange(n_own, dtype=jnp.int32)
    mine = lax.axis_index("own")
    stored = jnp.sum(jnp.where(owner == mine, block_ids, 0))
    up_all = lax.all_gather(up_weight, "own", axis=1, tiled=True)
    up_mine = lax.dynamic_slice_in_dim(up_all, stored * hid, hid, 1)
    whole = lax.all_gather(tokens, "own", axis=1, tiled=True)
    local = project(rms_rows(whole, gain), gate_weight, up_mine)
    local = jnp.where(live[:, None], local, 0)
    outgoing = jnp.where(filled[:, None], local[source], 0).reshape(n_req, pair, hid)
    packed = lax.all_to_all(outgoing, "req", split_axis=0, concat_axis=0, tiled=True).reshape(
        slots, hid
    )
    return (packed, local)


def solution(mesh):
    placed = (P("req", "own"), P(), P("req", "own"), P("req", "own"), P("req"), P("req"), P())
    return jax.shard_map(
        body,
        mesh=mesh,
        in_specs=placed,
        out_specs=(P("req", "own"), P("req", "own")),
        check_vma=False,
    )
```

profile of v0, /device:TPU:3, one launch (start us, length us, event | category | flops | bytes accessed | tf_op | source)
XLA Modules:
  0.0 511.1 jit_solution(7807440136936647943)
XLA Ops:
  7.2 0.0 copy-start.1
  7.2 0.0 all-gather.4.cloned.1.call-start
  7.2 0.7 all-gather.4.cloned.1.call-update
  7.9 0.0 all-gather.6.cloned.1.call-start
  8.0 0.7 all-gather.6.cloned.1.call-update
  8.7 0.0 all-gather.8.cloned.1.call-start
  8.7 1.3 fusion.32
  10.7 8.7 %all_gather.14 = bf16[256,1024]{1,0:T(8,128)(2,1)S(1)} all-gather(bf16[256,256]{1,0:T(8,128)(2,1)} %param.10), channel_id=1, replica_groups=mesh['req'=64,'own'=4] {'own'}, dimensions={1}, use_global_device_ids=true | all-gather | bytes 655360 | tf_op jit(solution)/shard_map/all_gather | solution.py:50
  19.3 0.7 constant_dynamic-slice_fusion
  20.0 0.0 all-gather.8.cloned.1.call-update
  20.0 0.7 fusion.23
  20.8 0.7 fusion.21
  21.5 1.2 reduce-window.6
  22.7 0.2 slice_reduce_fusion
  22.9 0.7 fusion.22
  23.7 0.8 fusion.18
  24.5 0.8 compare_select_fusion
  25.2 2.4 scatter_custom_fusion.1
  27.7 2.6 scatter_custom_fusion
  30.3 0.1 broadcast_in_dim.62
  30.5 135.3 %all-gather.4.cloned.1.call-done = bf16[512,16384]{1,0:T(8,128)(2,1)} async-done(((bf16[512,4096]{1,0:T(8,128)(2,1)}), bf16[512,16384]{1,0:T(8,128)(2,1)}) %all-gather.4.cloned.1.call-update) | async-done | bytes 16777232 | tf_op jit(solution)/shard_map/all_gather | solution.py:52
  165.8 7.2 %fusion = f32[512]{0:T(512)S(1)} fusion(bf16[512,16384]{1,0:T(8,128)(2,1)} %all-gather.4.cloned.1.call-done), kind=kLoop, calls=%fused_computation.5 | loop fusion | flops 25165312 | bytes 16779264 | tf_op jit(solution)/shard_map/reduce_sum | solution.py:11
  173.0 145.3 %all-gather.6.cloned.1.call-done = bf16[16384,256]{1,0:T(8,128)(2,1)} async-done(((bf16[256,256]{1,0:T(8,128)(2,1)}), bf16[16384,256]{1,0:T(8,128)(2,1)}) %all-gather.6.cloned.1.call-update) | async-done | bytes 8388624 | tf_op jit(solution)/shard_map/all_gather | solution.py:18
  318.4 0.0 copy-done.1
  318.4 10.7 %fusion.5 = f32[512,256]{1,0:T(8,128)S(1)} fusion(bf16[16384,256]{1,0:T(8,128)(2,1)} %all-gather.6.cloned.1.call-done, bf16[512,16384]{1,0:T(8,128)(2,1)} %all-gather.4.cloned.1.call-done, f32[16384]{0:T(1024)S(1)} %copy-done.1, f32[512]{0:T(512)S(1)} %add_rsqrt_fusion), kind=kOutput, calls=%fused_computation.9 | convolution fusion | flops 4328521728 | bytes 25757696 | tf_op jit(solution)/shard_map/dot_general | solution.py:16
  329.1 141.0 %all-gather.8.cloned.1.call-done = bf16[16384,256]{1,0:T(8,128)(2,1)} async-done(((bf16[256,256]{1,0:T(8,128)(2,1)}), bf16[16384,256]{1,0:T(8,128)(2,1)}) %all-gather.8.cloned.1.call-update) | async-done | bytes 8388624 | tf_op jit(solution)/shard_map/all_gather | solution.py:23
  470.0 12.7 %fusion.13 = bf16[512,256]{1,0:T(8,128)(2,1)S(1)} fusion(bf16[16384,256]{1,0:T(8,128)(2,1)} %all-gather.8.cloned.1.call-done, bf16[512,16384]{1,0:T(8,128)(2,1)} %all-gather.4.cloned.1.call-done, f32[16384]{0:T(1024)S(1)} %copy-done.1, f32[512]{0:T(512)S(1)} %add_rsqrt_fusion, f32[512,256]{1,0:T(8,128)S(1)} %fusion.5, pred[512]{0:T(512)(128)(4,1)S(1)} %fusion.22), kind=kOutput, calls=%fused_computation.12 | convolution fusion | flops 4329439232 | bytes 26020352 | tf_op jit(solution)/shard_map/dot_general | solution.py:21
  482.8 0.0 copy-start
  482.8 1.2 gather_fusion
  484.0 0.1 broadcast_select_fusion
  484.1 19.8 %all_to_all.5 = bf16[64,4,256]{2,1,0:T(4,128)(2,1)S(1)} all-to-all(bf16[64,4,256]{2,1,0:T(4,128)(2,1)S(1)} %broadcast_select_fusion), channel_id=1, replica_groups=mesh['req'=64,'own'=4] {'req'}, dimensions={0} | all-to-all | bytes 262144 | tf_op jit(solution)/shard_map/all_to_all | solution.py:56
  503.9 0.7 reshape.65
  (9 shorter events, 0.1 us)
Async XLA Ops:
  7.2 311.2 %copy-start.1 = (f32[16384]{0:T(1024)S(1)}, f32[16384]{0:T(1024)}, u32[]{:S(2)}) copy-start(f32[16384]{0:T(1024)} %param.8) | copy-start | bytes 196612
  7.2 158.6 %all-gather.4.cloned.1.call-start = ((), (), s32[]{:S(2)}) async-start(), calls=%async_computation.1 | async-start | bytes 20971520 | tf_op jit(solution)/shard_map/all_gather | solution.py:52
  7.9 310.4 %all-gather.6.cloned.1.call-start = ((), (), s32[]{:S(2)}) async-start(), calls=%async_computation.2 | async-start | bytes 8519680 | tf_op jit(solution)/shard_map/all_gather | solution.py:18
  8.7 461.4 %all-gather.8.cloned.1.call-start = ((), (), s32[]{:S(2)}) async-start(), calls=%async_computation.3 | async-start | bytes 8519680 | tf_op jit(solution)/shard_map/all_gather | solution.py:23
  482.8 21.8 %copy-start = (bf16[512,256]{1,0:T(8,128)(2,1)}, bf16[512,256]{1,0:T(8,128)(2,1)S(1)}, u32[]{:S(2)}) copy-start(bf16[512,256]{1,0:T(8,128)(2,1)S(1)} %fusion.13) | copy-start | bytes 786436
Sparse Core Ops, SparseCore 0:
  9.8 155.9 all-gather.3
  169.4 148.8 all-gather.5
  322.6 147.4 all-gather.7
where the time goes:
time: 515 us; the launch traced here: 511 us
  waiting for transfers between devices  423 us (82%)
  blocking collectives  28.4 us (6%)
  matrix products  23.4 us (5%)
  between operations  14.5 us (3%)
  other arithmetic  13.6 us (3%)
  local copies, waits for them, and re-layouts  7.98 us (2%)
    all_gather x1, waiting for transfers between devices, project(): lax.all_gather(gate_weight, 'req', axis=0, tiled=True)  145 us
    all_gather x1, waiting for transfers between devices, project(): lax.all_gather(up_mine, 'req', axis=0, tiled=True)  141 us
    all_gather x1, waiting for transfers between devices, body(): whole = lax.all_gather(tokens, 'own', axis=1, tiled=True)  135 us
    all_to_all x1, blocking collectives, body(): lax.all_to_all(outgoing, 'req', split_axis=0, concat_axis=0, tiled=True)  19.8 us
    dot_general x1, matrix products, project(): jnp.dot(normed, lax.all_gather(up_mine, 'req', axis=0, tiled=True), prefe...  12.7 us
    dot_general x1, matrix products, project(): jnp.dot(normed, lax.all_gather(gate_weight, 'req', axis=0, tiled=True), p...  10.7 us
  transfers between devices with their start and end apart: 3, of which 3 were waited for; matrix products, arithmetic and copies ran while one was open for 6% of the time, Pallas kernels for 0%

commit v1 on v0

v1 whole, which is shorter than its diff:
```python
import functools

import jax
import jax.numpy as jnp
from jax import lax
from jax.experimental import pallas as pl
from jax.experimental.pallas import tpu as pltpu
from jax.sharding import PartitionSpec as P

MESH = pl.DeviceIdType.MESH
f32 = jnp.float32
bf16 = jnp.bfloat16

norm_eps = 1e-05
D = 16384
N_REQ = 64
N_OWN = 4
NX, NY, NZ = 4, 4, 8
TOK = 512
ROWS = 256
HID = 256
FEAT = 4096
PAIR = 4
SUB = 1
NQ = N_OWN * SUB
HC = HID // SUB
WC = 2 * HC
CUT = 144
STREAM = 5 * NQ
HOP, RING_ON, RING_END, AHEAD, JOIN = 2, 2, 4, 4, 2
LAST = 4 * HOP + max(4, RING_END)


def kernel(
    gain, owner, lengths, dest, tok_hbm, gate_w, up_w,
    packed_out, local_out,
    tok, pick, act, act_out, panel, root_gate, root_up, squares, squares_in,
    part, part_in, red_out, red_in, hid, a2a_out, a2a_in, wide,
    s_tok, s_act, s_root_out, s_gate_in, s_up_in, s_sq_out, s_sq_in,
    s_chain_out, s_chain_in, s_ring_out, s_ring_in, s_edge_out, s_edge_in, s_spread_out, s_spread_in,
    s_part_out, s_part_in, s_red_out, s_red_in, s_a2a_out, s_a2a_in,
):
    req = lax.axis_index("req")
    own = lax.axis_index("own")
    h, z, y = req // 32, (req // 4) % 8, req % 4
    j, c = own // 2, own % 2
    x = 2 * h + j

    def at(x_, y_, z_, c_):
        x_, y_, z_ = lax.rem(x_ + NX, NX), lax.rem(y_ + NY, NY), lax.rem(z_ + NZ, NZ)
        return ((x_ // 2 * NZ + z_) * NY + y_, (x_ % 2) * 2 + c_)

    def remote(src, dst, send, recv, device):
        return pltpu.make_async_remote_copy(
            src_ref=src, dst_ref=dst, send_sem=send, recv_sem=recv, device_id=device, device_id_type=MESH
        )

    def arrived(ref, sem):
        pltpu.make_async_copy(ref, ref, sem).wait()


    barrier = pltpu.get_barrier_semaphore()

    def greet_req(i, _):
        pl.semaphore_signal(barrier, inc=1, device_id=(lax.rem(req + i, N_REQ), own), device_id_type=MESH)
        return 0

    lax.fori_loop(1, N_REQ, greet_req, 0)
    for k in range(1, N_OWN):
        peer = lax.rem(own + k, N_OWN)
        for other in (req, lax.rem(req + 32, N_REQ)):
            pl.semaphore_signal(barrier, inc=1, device_id=(other, peer), device_id_type=MESH)

    fetch = pltpu.make_async_copy(tok_hbm, tok, s_tok)
    fetch.start()

    slot = lax.broadcasted_iota(jnp.int32, (1, TOK), 1)
    span = jnp.where(
        slot < 128, lengths[0], jnp.where(slot < 256, lengths[1], jnp.where(slot < 384, lengths[2], lengths[3]))
    )
    live = (slot % 128) < span
    to = jnp.where(live, dest[...], -1)
    marks = (lax.broadcasted_iota(jnp.int32, (N_REQ, TOK), 0) == to).astype(f32)
    earlier = lax.broadcasted_iota(jnp.int32, (TOK, TOK), 0) < lax.broadcasted_iota(jnp.int32, (TOK, TOK), 1)
    before = jnp.dot(marks.astype(bf16), earlier.astype(f32).astype(bf16), preferred_element_type=f32)
    rank = jnp.sum(before * marks, axis=0, keepdims=True)
    row = jnp.where(live, rank * N_REQ + to.astype(f32), -1.0)
    pick[...] = (lax.broadcasted_iota(jnp.int32, (ROWS, TOK), 0).astype(f32) == row).astype(f32).astype(bf16)
    fetch.wait()

    mine = pl.ds(pl.multiple_of(h * ROWS, ROWS), ROWS)

    def arrange(block, out):
        col = pl.multiple_of(block * 1024, 1024)
        rows = jnp.dot(pick[...], tok[:, pl.ds(col, 1024)], preferred_element_type=f32)
        sq = rows * rows
        for k in range(8):
            squares[...] += sq[:, k * 128 : (k + 1) * 128]
        scaled = rows * gain[:, pl.ds(pl.multiple_of(own * FEAT + block * 1024, 1024), 1024)]
        out[...] = scaled.astype(bf16)

    squares[...] = jnp.zeros_like(squares)
    for zz in range(2):
        arrange(1 - h + 2 * zz, act_out.at[:, pl.ds(zz * 1024, 1024)])

    pl.semaphore_wait(barrier, N_REQ - 1 + 2 * (N_OWN - 1))

    root = at(2 * (z % 2) + h, y, z, z // 4)
    self_root = jnp.logical_and(2 * (z % 2) + h == x, z // 4 == c)

    @pl.when(self_root)
    def _():
        pltpu.make_async_copy(up_w, root_up.at[own], s_up_in.at[own]).start()
        pltpu.make_async_copy(gate_w, root_gate.at[own], s_gate_in.at[own]).start()

    @pl.when(jnp.logical_not(self_root))
    def _():
        remote(up_w, root_up.at[own], s_root_out.at[0], s_up_in.at[own], root).start()
        remote(gate_w, root_gate.at[own], s_root_out.at[1], s_gate_in.at[own], root).start()

    partner = (lax.rem(req + 32, N_REQ), own)
    give = remote(act_out, act.at[mine], s_act.at[0], s_act.at[1], partner)
    give.start()

    for zz in range(2):
        arrange(h + 2 * zz, act.at[mine, pl.ds(zz * 1024, 1024)])
    sq_sends = []
    for k in range(1, N_OWN):
        peer = lax.rem(own + k, N_OWN)
        cp = remote(squares, squares_in.at[k - 1], s_sq_out.at[k - 1], s_sq_in.at[k - 1], (req, peer))
        cp.start()
        sq_sends.append(cp)

    is_root = jnp.logical_and(z % 2 == h, z // 4 == c)
    zr = (z % 4) // 2

    def block(q, zz, yy, rows):
        return panel.at[q, zz, yy, pl.ds(rows[0], rows[1])]

    ra, rb = (0, CUT), (CUT, ROWS - CUT)

    def z_next(way):
        return at(x, y, z + 1 - 2 * way, c)

    def chain_copy(q, zz, way):
        ref = block(q, zz, y, ra)
        return remote(ref, ref, s_chain_out.at[q, zz, way], s_chain_in.at[q, zz], z_next(way))

    def spread_copy(q, zz, k, way):
        ref = block(q, zz, lax.rem(y + k, NY), rb)
        return remote(ref, ref, s_spread_out.at[q, zz, k, way], s_spread_in.at[q, zz, k], z_next(way))

    def y_copy(q, zz, k, rows, out, into, turn):
        way = turn if k == 2 else k
        yy = lax.rem(y + 3 - 2 * way, NY) if k == 2 else y
        ref = block(q, zz, yy, rows)
        return remote(ref, ref, out, into, at(x, y + 1 - 2 * way, z, c))

    def ring_copy(q, zz, k):
        return y_copy(q, zz, k, ra, s_ring_out.at[q, zz, k], s_ring_in.at[q, zz, k], zz)

    def edge_copy(q, k):
        return y_copy(q, zr, k, rb, s_edge_out.at[q, k], s_edge_in.at[q, k], lax.rem(q, 2))

    def y_arrived(q, zz, k, rows, into, turn):
        step = 2 if k == 2 else 3 - 2 * k
        arrived(block(q, zz, lax.rem(y + step, NY), rows), into)

    def reach(q, zz):
        d = lax.rem(z - (4 * c + h + 2 * zz) + 2 * NZ, NZ)
        far = 4 - lax.rem(q + zz, 2)
        return d, jnp.logical_and(d > 0, d < far), d >= far + 2

    def hops(zz):
        d = lax.rem(z - (4 * c + h + 2 * zz) + 2 * NZ, NZ)
        return jnp.minimum(d, NZ - d)

    def load_panel(q):
        @pl.when(q == 0)
        def _():
            for k in range(N_OWN):
                arrived(root_up.at[k], s_up_in.at[k])

        o, s = q // SUB, lax.rem(q, SUB)

        @pl.when(s == 0)
        def _():
            arrived(root_gate.at[o], s_gate_in.at[o])

        stored = jnp.int32(0)
        for k in range(1, N_OWN):
            stored = jnp.where(owner[k] == o, k, stored)
        cols = pl.ds(pl.multiple_of(s * HC, HC), HC)
        panel[q, zr, y, :, :HC] = root_gate[o, :, cols]
        panel[q, zr, y, :, HC:] = root_up[stored, :, cols]

    def open_edges(q):
        load_panel(q)
        for k in range(2):
            edge_copy(q, k).start()

    def on_chain(q, zz):
        d, up, down = reach(q, zz)

        @pl.when(d == 0)
        def _():
            @pl.when(q == 0)
            def _():
                open_edges(q)

            for way in range(2):
                chain_copy(q, zz, way).start()

        @pl.when(d > 0)
        def _():
            arrived(block(q, zz, y, ra), s_chain_in.at[q, zz])

            @pl.when(jnp.logical_or(up, down))
            def _():
                chain_copy(q, zz, down.astype(jnp.int32)).start()

        for k in range(2):
            ring_copy(q, zz, k).start()

    def on_spread(q, zz, i):
        k = jnp.where(i == 1, 0, jnp.where(i == 2, 3, jnp.where(i == 3, 1, 2)))
        d, up, down = reach(q, zz)

        @pl.when(d == 0)
        def _():
            @pl.when(i > 1)
            def _():
                arrived(block(q, zz, lax.rem(y + k, NY), rb), s_edge_in.at[q, i - 2])

                @pl.when(i == 2 + lax.rem(q, 2))
                def _():
                    edge_copy(q, 2).start()

            for way in range(2):
                spread_copy(q, zz, k, way).start()

            @pl.when(jnp.logical_and(i == AHEAD, q < NQ - 1))
            def _():
                open_edges(q + 1)

        @pl.when(d > 0)
        def _():
            arrived(block(q, zz, lax.rem(y + k, NY), rb), s_spread_in.at[q, zz, k])

            @pl.when(jnp.logical_or(up, down))
            def _():
                spread_copy(q, zz, k, down.astype(jnp.int32)).start()

    def flow(n, zz):
        @pl.when(jnp.logical_and(n >= 0, n < STREAM))
        def _():
            q = n // 5
            i = n - 5 * q

            @pl.when(i == 0)
            def _():
                on_chain(q, zz)

            @pl.when(i > 0)
            def _():
                on_spread(q, zz, i)

    def each_chunk(n, f):
        @pl.when(jnp.logical_and(jnp.logical_and(n >= 0, n < STREAM), lax.rem(n + 5 * 64, 5) == 0))
        def _():
            f(n // 5)

    def ring_on(zz, q):
        y_arrived(q, zz, zz, ra, s_ring_in.at[q, zz, zz], zz)
        ring_copy(q, zz, 2).start()

    def ring_end(zz, q):
        y_arrived(q, zz, 1 - zz, ra, s_ring_in.at[q, zz, 1 - zz], zz)
        y_arrived(q, zz, 2, ra, s_ring_in.at[q, zz, 2], zz)

    keep = pl.ds(pl.multiple_of(c * ROWS, ROWS), ROWS)
    pass_on = pl.ds(pl.multiple_of((1 - c) * ROWS, ROWS), ROWS)

    def part_copy(q):
        return remote(part.at[q, pass_on], part_in.at[q], s_part_out.at[q], s_part_in.at[q], (req, 2 * j + 1 - c))

    def dot(q):
        @pl.when(q == 0)
        def _():
            give.wait_recv()

        w = panel[q].reshape(8 * ROWS, WC)
        part[q] = jnp.dot(act[...], w, preferred_element_type=f32)
        part_copy(q).start()

    def red_to(q):
        o = q // SUB
        there = 2 * c + o // 2
        return at(there, y, z, o % 2), jnp.logical_and(there == x, o % 2 == c)

    def red_copy(q):
        device, _ = red_to(q)
        return remote(red_out.at[q], red_in.at[x, q % SUB], s_red_out.at[q], s_red_in.at[x, q % SUB], device)

    def total(q):
        arrived(part_in.at[q], s_part_in.at[q])
        _, here = red_to(q)
        both = (part[q, keep] + part_in[q]).astype(bf16)

        @pl.when(here)
        def _():
            red_in[x, q % SUB] = both

        @pl.when(jnp.logical_not(here))
        def _():
            red_out[q] = both
            red_copy(q).start()

    first = (hops(1) < hops(0)).astype(jnp.int32)

    def turn(t, _):
        for zz in (first, 1 - first):
            flow(t - HOP * hops(zz), zz)
        for zz in range(2):
            each_chunk(t - HOP * hops(zz) - RING_ON, functools.partial(ring_on, zz))
        for zz in range(2):
            each_chunk(t - HOP * hops(zz) - RING_END, functools.partial(ring_end, zz))
        each_chunk(t - LAST, dot)
        each_chunk(t - LAST - JOIN, total)
        return 0

    lax.fori_loop(0, STREAM - 4 + LAST + JOIN, turn, 0)

    for k in range(N_OWN - 1):
        arrived(squares_in.at[k], s_sq_in.at[k])
    sq = squares[...] + squares_in[0] + squares_in[1] + squares_in[2]
    scale = lax.rsqrt(jnp.sum(sq, axis=1, keepdims=True) * (1.0 / D) + norm_eps)

    for k in range(NX):
        @pl.when(jnp.logical_or(x != k, h != c))
        def _():
            for s in range(SUB):
                arrived(red_in.at[k, s], s_red_in.at[k, s])

    for s in range(SUB):
        both = red_in[0, s].astype(f32)
        for k in range(1, NX):
            both = both + red_in[k, s].astype(f32)
        gate = both[:, :HC] * scale
        up = both[:, HC:] * scale
        hid[:, s * HC : (s + 1) * HC] = (gate / (1.0 + jnp.exp(-gate)) * up).astype(bf16)

    for half in range(2):
        wide[...] = hid[:, half * 128 : (half + 1) * 128].astype(f32)
        for k in range(PAIR):
            a2a_out[pl.ds(half * PAIR + k, N_REQ, stride=8), :] = wide[k * N_REQ : (k + 1) * N_REQ, :]

    my_tile = pl.ds(pl.multiple_of(req * 8, 8), 8)

    def send_tile(i, _):
        to_req = lax.rem(req + i, N_REQ)
        src = a2a_out.at[pl.ds(pl.multiple_of(to_req * 8, 8), 8)]
        remote(src, a2a_in.at[my_tile], s_a2a_out, s_a2a_in, (to_req, own)).start()
        return 0

    lax.fori_loop(1, N_REQ, send_tile, 0)
    local_out[...] = lax.dot_general(
        pick[...], hid[...], (((0,), (0,)), ((), ())), preferred_element_type=f32
    ).astype(bf16)
    a2a_in[my_tile, :] = a2a_out[my_tile, :]

    def drain(q, _):
        for zz in range(2):
            d, up, down = reach(q, zz)
            for way, on in enumerate((up, down)):
                @pl.when(jnp.logical_or(d == 0, on))
                def _():
                    chain_copy(q, zz, way).wait_send()
                    for k in range(NY):
                        spread_copy(q, zz, k, way).wait_send()
            for k in range(3):
                ring_copy(q, zz, k).wait_send()

        @pl.when(is_root)
        def _():
            for k in range(3):
                edge_copy(q, k).wait_send()

        part_copy(q).wait_send()
        _, here = red_to(q)

        @pl.when(jnp.logical_not(here))
        def _():
            red_copy(q).wait_send()
        return 0

    lax.fori_loop(0, NQ, drain, 0)
    give.wait_send()
    for cp in sq_sends:
        cp.wait_send()

    @pl.when(jnp.logical_not(self_root))
    def _():
        remote(up_w, root_up.at[own], s_root_out.at[0], s_up_in.at[own], root).wait_send()
        remote(gate_w, root_gate.at[own], s_root_out.at[1], s_gate_in.at[own], root).wait_send()

    others = pl.ds(0, 8 * (N_REQ - 1))
    arrived(a2a_out.at[others], s_a2a_out)
    arrived(a2a_in.at[others], s_a2a_in)
    for half in range(2):
        for k in range(PAIR):
            wide[pl.ds(k, N_REQ, stride=PAIR), :] = a2a_in[pl.ds(half * PAIR + k, N_REQ, stride=8), :]
        packed_out[:, half * 128 : (half + 1) * 128] = wide[...].astype(bf16)


def body(tokens, gain, gate_weight, up_weight, lengths, dest, owner):
    vmem = pl.BlockSpec(memory_space=pltpu.VMEM)
    smem = pl.BlockSpec(memory_space=pltpu.SMEM)
    dma = pltpu.SemaphoreType.DMA
    return pl.pallas_call(
        kernel,
        out_shape=(jax.ShapeDtypeStruct((ROWS, HID), bf16), jax.ShapeDtypeStruct((TOK, HID), bf16)),
        in_specs=[vmem, smem, smem, vmem, pl.BlockSpec(memory_space=pl.ANY), vmem, vmem],
        out_specs=(vmem, vmem),
        scratch_shapes=[
            pltpu.VMEM((TOK, FEAT), bf16),
            pltpu.VMEM((ROWS, TOK), bf16),
            pltpu.VMEM((2 * ROWS, FEAT // 2), bf16),
            pltpu.VMEM((ROWS, FEAT // 2), bf16),
            pltpu.VMEM((NQ, 2, NY, ROWS, WC), bf16),
            pltpu.VMEM((N_OWN, ROWS, HID), bf16),
            pltpu.VMEM((N_OWN, ROWS, HID), bf16),
            pltpu.VMEM((ROWS, 128), f32),
            pltpu.VMEM((N_OWN - 1, ROWS, 128), f32),
            pltpu.VMEM((NQ, 2 * ROWS, WC), f32),
            pltpu.VMEM((NQ, ROWS, WC), f32),
            pltpu.VMEM((NQ, ROWS, WC), bf16),
            pltpu.VMEM((NX, SUB, ROWS, WC), bf16),
            pltpu.VMEM((ROWS, HID), bf16),
            pltpu.VMEM((8 * N_REQ, 128), f32),
            pltpu.VMEM((8 * N_REQ, 128), f32),
            pltpu.VMEM((ROWS, 128), f32),
            dma, dma((2,)), dma((2,)), dma((N_OWN,)), dma((N_OWN,)), dma((N_OWN - 1,)), dma((N_OWN - 1,)),
            dma((NQ, 2, 2)), dma((NQ, 2)), dma((NQ, 2, 3)), dma((NQ, 2, 3)), dma((NQ, 3)), dma((NQ, 3)),
            dma((NQ, 2, NY, 2)), dma((NQ, 2, NY)),
            dma((NQ,)), dma((NQ,)), dma((NQ,)), dma((NX, SUB)), dma, dma,
        ],
        compiler_params=pltpu.CompilerParams(
            collective_id=0, has_side_effects=True, vmem_limit_bytes=56 * 2**20
        ),
        name="swiglu_panel",
    )(gain.reshape(1, D), owner, lengths, dest.reshape(1, TOK), tokens, gate_weight, up_weight)


def solution(mesh):
    placed = (P("req", "own"), P(), P("req", "own"), P("req", "own"), P("req"), P("req"), P())
    return jax.shard_map(
        body,
        mesh=mesh,
        in_specs=placed,
        out_specs=(P("req", "own"), P("req", "own")),
        check_vma=False,
    )
```

time: 515 us -> 139 us (0.27)
  waiting for transfers between devices: 423 us -> 0 us
  Pallas kernels: 0 us -> 135 us
  blocking collectives: 28.4 us -> 0 us
  matrix products: 23.4 us -> 0 us
  between operations: 14.5 us -> 0.64 us
  other arithmetic: 13.6 us -> 0 us
    all_gather x3 -> x0, waiting for transfers between devices: 422 us -> none  [the longest x1 145 us: project(): lax.all_gather(gate_weight, 'req', axis=0, tiled=True)]
    pallas_call x0 -> x1, Pallas kernels: none -> 135 us  [body(): pl.pallas_call(kernel, out_shape=(jax.ShapeDtypeStruct((ROWS, HID), bf16)...]
    dot_general x2 -> x0, matrix products: 23.4 us -> none  [the longest x1 12.7 us: project(): jnp.dot(normed, lax.all_gather(up_mine, 'req', axis=0, tiled=True), prefe...]
    all_to_all x1 -> x0, blocking collectives: 19.8 us -> none  [body(): lax.all_to_all(outgoing, 'req', split_axis=0, concat_axis=0, tiled=True)]
    reduce_sum x3 -> x0, other arithmetic: 9.28 us -> none  [the longest x1 7.19 us: rms_rows(): scale = lax.rsqrt(jnp.mean(wide * wide, axis=-1, keepdims=True) + norm_eps)]
    all_gather x1 -> x0, blocking collectives: 8.68 us -> none  [body(): up_all = lax.all_gather(up_weight, 'own', axis=1, tiled=True)]
  transfers between devices with their start and end apart: 3 -> 0, of which waited for: 3 -> 0; matrix products, arithmetic and copies ran while one was open for 6% -> 0% of each run, Pallas kernels for 0% -> 0%
where the time goes in v1:
time: 139 us
  Pallas kernels  135 us (97%)
  local copies, waits for them, and re-layouts  3.24 us (2%)
    pallas_call x1, Pallas kernels, body(): pl.pallas_call(kernel, out_shape=(jax.ShapeDtypeStruct((ROWS, HID), bf16)...  135 us
    unnamed x2, local copies, waits for them, and re-layouts  3.24 us

profile of v1, /device:TPU:3, one launch (start us, length us, event | category | flops | bytes accessed | tf_op | source)
XLA Modules:
  0.0 139.1 jit_solution(35175932547137723)
XLA Ops:
  0.6 135.2 %swiglu_panel.1 = (bf16[256,256]{1,0:T(8,128)(2,1)}, bf16[512,256]{1,0:T(8,128)(2,1)}) custom-call(f32[1,16384]{1,0:T(1,128)} %bitcast.2, s32[4]{0:T(128)} %owner.1, s32[4]{0:T(128)} %lengths.1, s32[1,512]{1,0:T(1,128)} %bitcast.3, bf16[512,4096]{1,0:T(8,128)(2,1)} %tok_hbm.1, bf16[256,256]{1,0:T(8,128)(2,1)} %gate_w.1, bf16[256,256]{1,0:T(8,128)(2,1)} %up_w.1), custom_call_target="tpu_custom_call" | custom-call | tf_op jit(solution)/shard_map/swiglu_panel/pallas_call | solution.py:420
  135.8 1.6 %copy.11 = bf16[256,256]{1,0:T(8,128)(2,1)} copy(bf16[256,256]{1,0:T(8,128)(2,1)} %get-tuple-element.4) | data formatting | bytes 262144
  137.4 1.7 %copy.12 = bf16[512,256]{1,0:T(8,128)(2,1)} copy(bf16[512,256]{1,0:T(8,128)(2,1)} %get-tuple-element.5) | data formatting | bytes 524288

commit v2 on v1

v2 whole, which is shorter than its diff:
```python
import functools

import jax
import jax.numpy as jnp
from jax import lax
from jax.experimental import pallas as pl
from jax.experimental.pallas import tpu as pltpu
from jax.sharding import PartitionSpec as P

MESH = pl.DeviceIdType.MESH
f32 = jnp.float32
bf16 = jnp.bfloat16

norm_eps = 1e-05
D = 16384
N_REQ = 64
N_OWN = 4
NX, NY, NZ = 4, 4, 8
TOK = 512
ROWS = 256
HID = 256
FEAT = 4096
PAIR = 4
NQ = 4
WC = 2 * HID
CUT = 160
STREAM = 5 * NQ
HOP, RING_ON, RING_END, AHEAD, JOIN = 3, 3, 5, 4, 2
GATES_T, UPS_T, GIVE_T, NORM_T, RELAY_T = 1, 2, 5, 7, 2
LAST = 4 * HOP + max(4, RING_END)


def kernel(
    gain, owner, lengths, dest, tok_hbm, gate_w, up_w,
    packed_out, local_hbm,
    tok, pick, act, act_out, panel, root_up, squares, squares_out, squares_in,
    part, part_in, red_out, red_in, hid, local_out, a2a_out, a2a_in, wide,
    s_tok, s_act, s_root_out, s_gate_in, s_up_in, s_sq_out, s_sq_in,
    s_chain_out, s_chain_in, s_ring_out, s_ring_in, s_edge_out, s_edge_in, s_spread_out, s_spread_in,
    s_part_out, s_part_in, s_red_out, s_red_in, s_a2a_out, s_a2a_in, s_local, relay,
):
    req = lax.axis_index("req")
    own = lax.axis_index("own")
    h, z, y = req // 32, (req // 4) % 8, req % 4
    j, c = own // 2, own % 2
    x = 2 * h + j

    def at(x_, y_, z_, c_):
        x_, y_, z_ = lax.rem(x_ + NX, NX), lax.rem(y_ + NY, NY), lax.rem(z_ + NZ, NZ)
        return ((x_ // 2 * NZ + z_) * NY + y_, (x_ % 2) * 2 + c_)

    def remote(src, dst, send, recv, device):
        return pltpu.make_async_remote_copy(
            src_ref=src, dst_ref=dst, send_sem=send, recv_sem=recv, device_id=device, device_id_type=MESH
        )

    def arrived(ref, sem):
        pltpu.make_async_copy(ref, ref, sem).wait()


    barrier = pltpu.get_barrier_semaphore()
    other_req = lax.rem(req + 32, N_REQ)
    beside = [at(x, y + 1, z, c), at(x, y - 1, z, c)], [at(x, y, z + 1, c), at(x, y, z - 1, c)]
    line = [(req, lax.rem(own + k, N_OWN)) for k in range(1, N_OWN)]
    line += [(other_req, lax.rem(own + k, N_OWN)) for k in range(N_OWN)]
    for device in line + beside[0] + beside[1]:
        pl.semaphore_signal(barrier, inc=1, device_id=device, device_id_type=MESH)

    fetch = pltpu.make_async_copy(tok_hbm, tok, s_tok)
    fetch.start()
    pl.semaphore_wait(barrier, 11)

    def pass_word(i):
        if i > 0:
            pl.semaphore_wait(relay.at[i - 1], 2)
        if i < 6:
            for device in beside[0 if i < 2 else 1]:
                pl.semaphore_signal(relay.at[i], inc=1, device_id=device, device_id_type=MESH)

    root = at(2 * (z % 2) + h, y, z, z // 4)
    self_root = jnp.logical_and(2 * (z % 2) + h == x, z // 4 == c)
    is_root = jnp.logical_and(z % 2 == h, z // 4 == c)
    zr = (z % 4) // 2

    def gate_at(k):
        return panel.at[k // 2, zr, y, :, pl.ds(pl.multiple_of(k % 2 * HID, HID), HID)]

    def to_root(src, dst, out, into):
        @pl.when(self_root)
        def _():
            pltpu.make_async_copy(src, dst, into).start()

        @pl.when(jnp.logical_not(self_root))
        def _():
            remote(src, dst, out, into, root).start()

    def gates_to_root():
        to_root(gate_w, gate_at(own), s_root_out.at[0], s_gate_in.at[own])

    def ups_to_root():
        to_root(up_w, root_up.at[own], s_root_out.at[1], s_up_in.at[own])

    gates_to_root()
    ups_to_root()

    pass_word(0)

    slot = lax.broadcasted_iota(jnp.int32, (1, TOK), 1)
    span = jnp.where(
        slot < 128, lengths[0], jnp.where(slot < 256, lengths[1], jnp.where(slot < 384, lengths[2], lengths[3]))
    )
    live = (slot % 128) < span
    to = jnp.where(live, dest[...], -1)
    marks = (lax.broadcasted_iota(jnp.int32, (N_REQ, TOK), 0) == to).astype(f32)
    earlier = lax.broadcasted_iota(jnp.int32, (TOK, TOK), 0) < lax.broadcasted_iota(jnp.int32, (TOK, TOK), 1)
    before = jnp.dot(marks.astype(bf16), earlier.astype(f32).astype(bf16), preferred_element_type=f32)
    rank = jnp.sum(before * marks, axis=0, keepdims=True)
    row = jnp.where(live, rank * N_REQ + to.astype(f32), -1.0)
    pick[...] = (lax.broadcasted_iota(jnp.int32, (ROWS, TOK), 0).astype(f32) == row).astype(f32).astype(bf16)
    fetch.wait()

    mine = pl.ds(pl.multiple_of(h * ROWS, ROWS), ROWS)

    def arrange(block, out):
        col = pl.multiple_of(block * 1024, 1024)
        rows = jnp.dot(pick[...], tok[:, pl.ds(col, 1024)], preferred_element_type=f32)
        sq = rows * rows
        for k in range(8):
            squares[...] += sq[:, k * 128 : (k + 1) * 128]
        out[...] = rows.astype(bf16)

    squares[...] = jnp.zeros_like(squares)
    for zz in range(2):
        arrange(1 - h + 2 * zz, act_out.at[:, pl.ds(zz * 1024, 1024)])
    for zz in range(2):
        arrange(h + 2 * zz, act.at[mine, pl.ds(zz * 1024, 1024)])

    partner = (other_req, own)
    give = remote(act_out, act.at[mine], s_act.at[0], s_act.at[1], partner)

    def turned(a, axis):
        eye = lax.broadcasted_iota(jnp.int32, (ROWS, ROWS), 0) == lax.broadcasted_iota(jnp.int32, (ROWS, ROWS), 1)
        return jnp.sum(jnp.where(eye, a, 0.0), axis=axis, keepdims=True)

    row_sums = turned(jnp.sum(squares[...], axis=1, keepdims=True), 0)
    squares_out[...] = jnp.broadcast_to(row_sums, (8, ROWS))
    sq_sends = []
    for k, device in enumerate(line):
        cp = remote(squares_out, squares_in.at[2 * own + h], s_sq_out.at[k], s_sq_in.at[2 * own + h], device)
        cp.start()
        sq_sends.append(cp)
    squares_in[2 * own + h] = squares_out[...]

    def normalize(hh):
        sums = squares_in[hh, 0:1, :]
        for k in range(1, N_OWN):
            sums = sums + squares_in[2 * k + hh, 0:1, :]
        scale = lax.rsqrt(turned(sums, 1) * (1.0 / D) + norm_eps)
        rows = pl.ds(pl.multiple_of(hh * ROWS, ROWS), ROWS)
        for zz in range(2):
            for n in range(2):
                cols = pl.ds(zz * 1024 + n * 512, 512)
                here = pl.multiple_of(own * FEAT + (h + 2 * zz) * 1024 + n * 512, 512)
                act[rows, cols] = (act[rows, cols].astype(f32) * scale * gain[:, pl.ds(here, 512)]).astype(bf16)

    def block(q, zz, yy, rows):
        return panel.at[q, zz, yy, pl.ds(rows[0], rows[1])]

    ra, rb = (0, CUT), (CUT, ROWS - CUT)

    def z_next(way):
        return at(x, y, z + 1 - 2 * way, c)

    def chain_copy(q, zz, way):
        ref = block(q, zz, y, ra)
        return remote(ref, ref, s_chain_out.at[q, zz, way], s_chain_in.at[q, zz], z_next(way))

    def spread_copy(q, zz, k, way):
        ref = block(q, zz, lax.rem(y + k, NY), rb)
        return remote(ref, ref, s_spread_out.at[q, zz, k, way], s_spread_in.at[q, zz, k], z_next(way))

    def y_copy(q, zz, k, rows, out, into, turn):
        way = turn if k == 2 else k
        yy = lax.rem(y + 3 - 2 * way, NY) if k == 2 else y
        ref = block(q, zz, yy, rows)
        return remote(ref, ref, out, into, at(x, y + 1 - 2 * way, z, c))

    def ring_copy(q, zz, k):
        return y_copy(q, zz, k, ra, s_ring_out.at[q, zz, k], s_ring_in.at[q, zz, k], zz)

    def edge_copy(q, k):
        return y_copy(q, zr, k, rb, s_edge_out.at[q, k], s_edge_in.at[q, k], lax.rem(q, 2))

    def y_arrived(q, zz, k, rows, into, turn):
        step = 2 if k == 2 else 3 - 2 * k
        arrived(block(q, zz, lax.rem(y + step, NY), rows), into)

    def reach(q, zz):
        d = lax.rem(z - (4 * c + h + 2 * zz) + 2 * NZ, NZ)
        far = 4 - lax.rem(q + zz, 2)
        return d, jnp.logical_and(d > 0, d < far), d >= far + 2

    def hops(zz):
        d = lax.rem(z - (4 * c + h + 2 * zz) + 2 * NZ, NZ)
        return jnp.minimum(d, NZ - d)

    def load_panel(q):
        @pl.when(q < 2)
        def _():
            for k in range(2):
                arrived(gate_at(2 * q + k), s_gate_in.at[2 * q + k])

        @pl.when(q == 2)
        def _():
            for k in range(N_OWN):
                arrived(root_up.at[k], s_up_in.at[k])

        @pl.when(q >= 2)
        def _():
            for k in range(2):
                stored = jnp.int32(0)
                for m in range(1, N_OWN):
                    stored = jnp.where(owner[m] == 2 * (q - 2) + k, m, stored)
                panel[q, zr, y, :, k * HID : (k + 1) * HID] = root_up[stored]

    def open_edges(q):
        load_panel(q)
        for k in range(2):
            edge_copy(q, k).start()

    def on_chain(q, zz):
        d, up, down = reach(q, zz)

        @pl.when(d == 0)
        def _():
            @pl.when(q == 0)
            def _():
                open_edges(q)

            for way in range(2):
                chain_copy(q, zz, way).start()

        @pl.when(d > 0)
        def _():
            arrived(block(q, zz, y, ra), s_chain_in.at[q, zz])

            @pl.when(jnp.logical_or(up, down))
            def _():
                chain_copy(q, zz, down.astype(jnp.int32)).start()

        for k in range(2):
            ring_copy(q, zz, k).start()

    def on_spread(q, zz, i):
        k = jnp.where(i == 1, 0, jnp.where(i == 2, 3, jnp.where(i == 3, 1, 2)))
        d, up, down = reach(q, zz)

        @pl.when(d == 0)
        def _():
            @pl.when(i > 1)
            def _():
                arrived(block(q, zz, lax.rem(y + k, NY), rb), s_edge_in.at[q, i - 2])

                @pl.when(i == 2 + lax.rem(q, 2))
                def _():
                    edge_copy(q, 2).start()

            for way in range(2):
                spread_copy(q, zz, k, way).start()

            @pl.when(jnp.logical_and(i == AHEAD, q < NQ - 1))
            def _():
                open_edges(q + 1)

        @pl.when(d > 0)
        def _():
            arrived(block(q, zz, lax.rem(y + k, NY), rb), s_spread_in.at[q, zz, k])

            @pl.when(jnp.logical_or(up, down))
            def _():
                spread_copy(q, zz, k, down.astype(jnp.int32)).start()

    def flow(n, zz):
        @pl.when(jnp.logical_and(n >= 0, n < STREAM))
        def _():
            q = n // 5
            i = n - 5 * q

            @pl.when(i == 0)
            def _():
                on_chain(q, zz)

            @pl.when(i > 0)
            def _():
                on_spread(q, zz, i)

    def each_chunk(n, f):
        @pl.when(jnp.logical_and(jnp.logical_and(n >= 0, n < STREAM), lax.rem(n + 5 * 64, 5) == 0))
        def _():
            f(n // 5)

    def ring_on(zz, q):
        y_arrived(q, zz, zz, ra, s_ring_in.at[q, zz, zz], zz)
        ring_copy(q, zz, 2).start()

    def ring_end(zz, q):
        y_arrived(q, zz, 1 - zz, ra, s_ring_in.at[q, zz, 1 - zz], zz)
        y_arrived(q, zz, 2, ra, s_ring_in.at[q, zz, 2], zz)

    keep = pl.ds(pl.multiple_of(c * ROWS, ROWS), ROWS)
    pass_on = pl.ds(pl.multiple_of((1 - c) * ROWS, ROWS), ROWS)

    def part_copy(q, k):
        return remote(
            part.at[q, k, pass_on], part_in.at[q, k], s_part_out.at[q, k], s_part_in.at[q, k], (req, 2 * j + 1 - c)
        )

    def dot(q):
        for k in range(2):
            w = panel[q, :, :, :, k * HID : (k + 1) * HID].reshape(8 * ROWS, HID)
            part[q, k] = jnp.dot(act[...], w, preferred_element_type=f32)
            part_copy(q, k).start()

    def red_copy(q, k):
        device = at(2 * c + lax.rem(q, 2), y, z, k)
        return remote(red_out.at[q, k], red_in.at[x, q // 2], s_red_out.at[q, k], s_red_in.at[x, q // 2], device)

    def red_here(q, k):
        return jnp.logical_and(2 * c + lax.rem(q, 2) == x, c == k)

    def total(q):
        for k in range(2):
            arrived(part_in.at[q, k], s_part_in.at[q, k])
            both = (part[q, k, keep] + part_in[q, k]).astype(bf16)
            here = red_here(q, k)

            @pl.when(here)
            def _():
                red_in[x, q // 2] = both

            @pl.when(jnp.logical_not(here))
            def _():
                red_out[q, k] = both
                red_copy(q, k).start()

        for zz in range(2):
            d, up, down = reach(q, zz)
            for way, on in enumerate((up, down)):
                @pl.when(jnp.logical_or(d == 0, on))
                def _():
                    chain_copy(q, zz, way).wait_send()
                    for k in range(NY):
                        spread_copy(q, zz, k, way).wait_send()
            for k in range(3):
                ring_copy(q, zz, k).wait_send()

        @pl.when(is_root)
        def _():
            for k in range(3):
                edge_copy(q, k).wait_send()

        for k in range(2):
            part_copy(q, k).wait_send()

    first = (hops(1) < hops(0)).astype(jnp.int32)

    def once(t, when, f, *args):
        @pl.when(t == when)
        def _():
            f(*args)

    def normalize_given():
        give.wait_recv()
        normalize(1 - h)

    def normalize_mine():
        for k in range(1, 8):
            slot = lax.rem(2 * own + h + k, 8)
            arrived(squares_in.at[slot], s_sq_in.at[slot])
        normalize(h)

    def turn(t, _):
        once(t, HOP * jnp.minimum(hops(0), hops(1)) + GIVE_T, give.start)
        for i in range(1, 7):
            once(t, i * RELAY_T, pass_word, i)
        for zz in (first, 1 - first):
            flow(t - HOP * hops(zz), zz)
        for zz in range(2):
            each_chunk(t - HOP * hops(zz) - RING_ON, functools.partial(ring_on, zz))
        for zz in range(2):
            each_chunk(t - HOP * hops(zz) - RING_END, functools.partial(ring_end, zz))
        once(t, NORM_T, normalize_mine)
        once(t, LAST - 1, normalize_given)
        each_chunk(t - LAST, dot)
        each_chunk(t - LAST - JOIN, total)
        return 0

    lax.fori_loop(0, STREAM - 4 + LAST + JOIN, turn, 0)

    for k in range(NX):
        @pl.when(jnp.logical_or(x != k, h != c))
        def _():
            for kind in range(2):
                arrived(red_in.at[k, kind], s_red_in.at[k, kind])

    def joined(kind):
        both = red_in[0, kind].astype(f32)
        for k in range(1, NX):
            both = both + red_in[k, kind].astype(f32)
        return both

    gate = joined(0)
    hid[...] = (gate / (1.0 + jnp.exp(-gate)) * joined(1)).astype(bf16)

    for half in range(2):
        wide[...] = hid[:, half * 128 : (half + 1) * 128].astype(f32)
        for k in range(PAIR):
            a2a_out[pl.ds(half * PAIR + k, N_REQ, stride=8), :] = wide[k * N_REQ : (k + 1) * N_REQ, :]

    my_tile = pl.ds(pl.multiple_of(req * 8, 8), 8)

    def send_tile(i, _):
        to_req = lax.rem(req + i, N_REQ)
        src = a2a_out.at[pl.ds(pl.multiple_of(to_req * 8, 8), 8)]
        remote(src, a2a_in.at[my_tile], s_a2a_out, s_a2a_in, (to_req, own)).start()
        return 0

    lax.fori_loop(1, N_REQ, send_tile, 0)
    local_out[...] = lax.dot_general(
        pick[...], hid[...], (((0,), (0,)), ((), ())), preferred_element_type=f32
    ).astype(bf16)
    keep_local = pltpu.make_async_copy(local_out, local_hbm, s_local)
    keep_local.start()
    a2a_in[my_tile, :] = a2a_out[my_tile, :]

    for q in range(NQ):
        for k in range(2):
            @pl.when(jnp.logical_not(red_here(q, k)))
            def _():
                red_copy(q, k).wait_send()
    give.wait_send()
    for cp in sq_sends:
        cp.wait_send()

    @pl.when(jnp.logical_not(self_root))
    def _():
        remote(gate_w, gate_at(own), s_root_out.at[0], s_gate_in.at[own], root).wait_send()
        remote(up_w, root_up.at[own], s_root_out.at[1], s_up_in.at[own], root).wait_send()

    others = pl.ds(0, 8 * (N_REQ - 1))
    arrived(a2a_out.at[others], s_a2a_out)
    arrived(a2a_in.at[others], s_a2a_in)
    for half in range(2):
        for k in range(PAIR):
            wide[pl.ds(k, N_REQ, stride=PAIR), :] = a2a_in[pl.ds(half * PAIR + k, N_REQ, stride=8), :]
        packed_out[:, half * 128 : (half + 1) * 128] = wide[...].astype(bf16)
    keep_local.wait()


def body(tokens, gain, gate_weight, up_weight, lengths, dest, owner):
    vmem = pl.BlockSpec(memory_space=pltpu.VMEM)
    smem = pl.BlockSpec(memory_space=pltpu.SMEM)
    dma = pltpu.SemaphoreType.DMA
    return pl.pallas_call(
        kernel,
        out_shape=(jax.ShapeDtypeStruct((ROWS, HID), bf16), jax.ShapeDtypeStruct((TOK, HID), bf16)),
        in_specs=[vmem, smem, smem, vmem, pl.BlockSpec(memory_space=pl.ANY), vmem, vmem],
        out_specs=(vmem, pl.BlockSpec(memory_space=pl.ANY)),
        scratch_shapes=[
            pltpu.VMEM((TOK, FEAT), bf16),
            pltpu.VMEM((ROWS, TOK), bf16),
            pltpu.VMEM((2 * ROWS, FEAT // 2), bf16),
            pltpu.VMEM((ROWS, FEAT // 2), bf16),
            pltpu.VMEM((NQ, 2, NY, ROWS, WC), bf16),
            pltpu.VMEM((N_OWN, ROWS, HID), bf16),
            pltpu.VMEM((ROWS, 128), f32),
            pltpu.VMEM((8, ROWS), f32),
            pltpu.VMEM((8, 8, ROWS), f32),
            pltpu.VMEM((NQ, 2, 2 * ROWS, HID), f32),
            pltpu.VMEM((NQ, 2, ROWS, HID), f32),
            pltpu.VMEM((NQ, 2, ROWS, HID), bf16),
            pltpu.VMEM((NX, 2, ROWS, HID), bf16),
            pltpu.VMEM((ROWS, HID), bf16),
            pltpu.VMEM((TOK, HID), bf16),
            pltpu.VMEM((8 * N_REQ, 128), f32),
            pltpu.VMEM((8 * N_REQ, 128), f32),
            pltpu.VMEM((ROWS, 128), f32),
            dma, dma((2,)), dma((2,)), dma((N_OWN,)), dma((N_OWN,)), dma((7,)), dma((8,)),
            dma((NQ, 2, 2)), dma((NQ, 2)), dma((NQ, 2, 3)), dma((NQ, 2, 3)), dma((NQ, 3)), dma((NQ, 3)),
            dma((NQ, 2, NY, 2)), dma((NQ, 2, NY)),
            dma((NQ, 2)), dma((NQ, 2)), dma((NQ, 2)), dma((NX, 2)), dma, dma, dma,
            pltpu.SemaphoreType.REGULAR((6,)),
        ],
        compiler_params=pltpu.CompilerParams(
            collective_id=0, has_side_effects=True, vmem_limit_bytes=56 * 2**20
        ),
        name="swiglu_panel",
    )(gain.reshape(1, D), owner, lengths, dest.reshape(1, TOK), tokens, gate_weight, up_weight)


def solution(mesh):
    placed = (P("req", "own"), P(), P("req", "own"), P("req", "own"), P("req"), P("req"), P())
    return jax.shard_map(
        body,
        mesh=mesh,
        in_specs=placed,
        out_specs=(P("req", "own"), P("req", "own")),
        check_vma=False,
    )
```

time: 139 us -> 112 us (0.81)
  Pallas kernels: 135 us -> 108 us
    pallas_call x1, Pallas kernels: 135 us -> 108 us  [body(): pl.pallas_call(kernel, out_shape=(jax.ShapeDtypeStruct((ROWS, HID), bf16)...]
where the time goes in v2:
time: 112 us
  Pallas kernels  108 us (96%)
  local copies, waits for them, and re-layouts  3.24 us (3%)
    pallas_call x1, Pallas kernels, body(): pl.pallas_call(kernel, out_shape=(jax.ShapeDtypeStruct((ROWS, HID), bf16)...  108 us
    unnamed x2, local copies, waits for them, and re-layouts  3.24 us

profile of v2, /device:TPU:3, one launch (start us, length us, event | category | flops | bytes accessed | tf_op | source)
XLA Modules:
  0.0 112.0 jit_solution(10532352532764390306)
XLA Ops:
  0.6 108.1 %swiglu_panel.1 = (bf16[256,256]{1,0:T(8,128)(2,1)}, bf16[512,256]{1,0:T(8,128)(2,1)}) custom-call(f32[1,16384]{1,0:T(1,128)} %bitcast.2, s32[4]{0:T(128)} %owner.1, s32[4]{0:T(128)} %lengths.1, s32[1,512]{1,0:T(1,128)} %bitcast.3, bf16[512,4096]{1,0:T(8,128)(2,1)} %tok_hbm.1, bf16[256,256]{1,0:T(8,128)(2,1)} %gate_w.1, bf16[256,256]{1,0:T(8,128)(2,1)} %up_w.1), custom_call_target="tpu_custom_call" | custom-call | tf_op jit(solution)/shard_map/swiglu_panel/pallas_call | solution.py:464
  108.8 1.6 %copy.11 = bf16[256,256]{1,0:T(8,128)(2,1)} copy(bf16[256,256]{1,0:T(8,128)(2,1)} %get-tuple-element.4) | data formatting | bytes 262144
  110.3 1.7 %copy.12 = bf16[512,256]{1,0:T(8,128)(2,1)} copy(bf16[512,256]{1,0:T(8,128)(2,1)} %get-tuple-element.5) | data formatting | bytes 524288

commit v3 on v2

--- a/solution.py
+++ b/solution.py
@@ -24,10 +24,20 @@
 NQ = 4
 WC = 2 * HID
 CUT = 160
+CHAIN_T = (1, 3, 9, 11)
+EDGE_T = (0, 4, 5, 9)
+ORDER = (0, 3, 1, 2)
+LAGS = (0, 4, 6, 10, 11)
+RING_ON, RING_END, JOIN, GIVE_T, RELAY_T = 4, 8, 2, 8, 2
 STREAM = 5 * NQ
-HOP, RING_ON, RING_END, AHEAD, JOIN = 3, 3, 5, 4, 2
-GATES_T, UPS_T, GIVE_T, NORM_T, RELAY_T = 1, 2, 5, 7, 2
-LAST = 4 * HOP + max(4, RING_END)
+LOAD_T = tuple(min(a, b) for a, b in zip(CHAIN_T, EDGE_T))
+REST_T = [n for n in range(STREAM) if n not in CHAIN_T]
+DOT_WAIT = (0, 0, 0, 0)
+DOT_T = tuple(LAGS[4] + max(REST_T[4 * q + 3], CHAIN_T[q] + RING_END) + DOT_WAIT[q] for q in range(NQ))
+TOTAL_T = [DOT_T[1] + 1]
+for done in DOT_T[2:]:
+    TOTAL_T.append(max(TOTAL_T[-1] + 1, done))
+TOTAL_T.append(TOTAL_T[-1] + 1)
 
 
 def kernel(
@@ -101,7 +111,6 @@
         to_root(up_w, root_up.at[own], s_root_out.at[1], s_up_in.at[own])
 
     gates_to_root()
-    ups_to_root()
 
     pass_word(0)
 
@@ -224,7 +233,6 @@
                 panel[q, zr, y, :, k * HID : (k + 1) * HID] = root_up[stored]
 
     def open_edges(q):
-        load_panel(q)
         for k in range(2):
             edge_copy(q, k).start()
 
@@ -233,10 +241,6 @@
 
         @pl.when(d == 0)
         def _():
-            @pl.when(q == 0)
-            def _():
-                open_edges(q)
-
             for way in range(2):
                 chain_copy(q, zz, way).start()
 
@@ -252,26 +256,23 @@
             ring_copy(q, zz, k).start()
 
     def on_spread(q, zz, i):
-        k = jnp.where(i == 1, 0, jnp.where(i == 2, 3, jnp.where(i == 3, 1, 2)))
+        k = pick_from(ORDER, i)
         d, up, down = reach(q, zz)
 
         @pl.when(d == 0)
         def _():
-            @pl.when(i > 1)
-            def _():
-                arrived(block(q, zz, lax.rem(y + k, NY), rb), s_edge_in.at[q, i - 2])
-
-                @pl.when(i == 2 + lax.rem(q, 2))
+            @pl.when(k > 0)
+            def _():
+                e = jnp.where(k == 3, 0, k)
+                arrived(block(q, zz, lax.rem(y + k, NY), rb), s_edge_in.at[q, e])
+
+                @pl.when(e == lax.rem(q, 2))
                 def _():
                     edge_copy(q, 2).start()
 
             for way in range(2):
                 spread_copy(q, zz, k, way).start()
 
-            @pl.when(jnp.logical_and(i == AHEAD, q < NQ - 1))
-            def _():
-                open_edges(q + 1)
-
         @pl.when(d > 0)
         def _():
             arrived(block(q, zz, lax.rem(y + k, NY), rb), s_spread_in.at[q, zz, k])
@@ -279,25 +280,48 @@
             @pl.when(jnp.logical_or(up, down))
             def _():
                 spread_copy(q, zz, k, down.astype(jnp.int32)).start()
+
+    def pick_from(table, i):
+        out = jnp.int32(table[0])
+        for k in range(1, len(table)):
+            out = jnp.where(i >= k, table[k], out)
+        return out
+
+    def which(n, table):
+        n_before, hit = jnp.int32(0), n == table[0]
+        for v in table:
+            n_before = n_before + (n > v).astype(jnp.int32)
+            hit = jnp.logical_or(hit, n == v)
+        return n_before, hit
 
     def flow(n, zz):
         @pl.when(jnp.logical_and(n >= 0, n < STREAM))
         def _():
-            q = n // 5
-            i = n - 5 * q
-
-            @pl.when(i == 0)
+            @pl.when(jnp.logical_and(is_root, zr == zz))
+            def _():
+                for table, f in ((LOAD_T, load_panel), (EDGE_T, open_edges)):
+                    q, hit = which(n, table)
+
+                    @pl.when(hit)
+                    def _():
+                        f(q)
+
+            q, hit = which(n, CHAIN_T)
+
+            @pl.when(hit)
             def _():
                 on_chain(q, zz)
 
-            @pl.when(i > 0)
-            def _():
-                on_spread(q, zz, i)
-
-    def each_chunk(n, f):
-        @pl.when(jnp.logical_and(jnp.logical_and(n >= 0, n < STREAM), lax.rem(n + 5 * 64, 5) == 0))
-        def _():
-            f(n // 5)
+            @pl.when(jnp.logical_not(hit))
+            def _():
+                on_spread((n - q) // 4, zz, lax.rem(n - q, 4))
+
+    def each_chunk(n, table, f):
+        q, hit = which(n, table)
+
+        @pl.when(hit)
+        def _():
+            f(q)
 
     def ring_on(zz, q):
         y_arrived(q, zz, zz, ra, s_ring_in.at[q, zz, zz], zz)
@@ -379,23 +403,33 @@
             arrived(squares_in.at[slot], s_sq_in.at[slot])
         normalize(h)
 
+    behind = [pick_from(LAGS, hops(zz)) for zz in range(2)]
+    near = jnp.minimum(behind[0], behind[1])
+
+    ups_to_root()
+
     def turn(t, _):
-        once(t, HOP * jnp.minimum(hops(0), hops(1)) + GIVE_T, give.start)
+        once(t, near + GIVE_T, give.start)
         for i in range(1, 7):
             once(t, i * RELAY_T, pass_word, i)
+
         for zz in (first, 1 - first):
-            flow(t - HOP * hops(zz), zz)
+            flow(t - jnp.where(zz == 0, behind[0], behind[1]), zz)
         for zz in range(2):
-            each_chunk(t - HOP * hops(zz) - RING_ON, functools.partial(ring_on, zz))
+            each_chunk(t - behind[zz] - RING_ON, CHAIN_T, functools.partial(ring_on, zz))
         for zz in range(2):
-            each_chunk(t - HOP * hops(zz) - RING_END, functools.partial(ring_end, zz))
-        once(t, NORM_T, normalize_mine)
-        once(t, LAST - 1, normalize_given)
-        each_chunk(t - LAST, dot)
-        each_chunk(t - LAST - JOIN, total)
+            each_chunk(t - behind[zz] - RING_END, CHAIN_T, functools.partial(ring_end, zz))
+
+        @pl.when(t == DOT_T[0] - 1)
+        def _():
+            normalize_mine()
+            normalize_given()
+
+        each_chunk(t, DOT_T, dot)
+        each_chunk(t, TOTAL_T, total)
         return 0
 
-    lax.fori_loop(0, STREAM - 4 + LAST + JOIN, turn, 0)
+    lax.fori_loop(0, TOTAL_T[-1] + 1, turn, 0)
 
     for k in range(NX):
         @pl.when(jnp.logical_or(x != k, h != c))

time: 112 us -> 110 us (0.982); the launches traced: 112 us -> 108 us
  Pallas kernels: 108 us -> 105 us
    pallas_call x1, Pallas kernels: 108 us -> 105 us  [body(): pl.pallas_call(kernel, out_shape=(jax.ShapeDtypeStruct((ROWS, HID), bf16)...]
where the time goes in v3:
time: 110 us; the launch traced here: 108 us
  Pallas kernels  105 us (95%)
  local copies, waits for them, and re-layouts  3.24 us (3%)
    pallas_call x1, Pallas kernels, body(): pl.pallas_call(kernel, out_shape=(jax.ShapeDtypeStruct((ROWS, HID), bf16)...  105 us
    unnamed x2, local copies, waits for them, and re-layouts  3.24 us

profile of v3, /device:TPU:3, one launch (start us, length us, event | category | flops | bytes accessed | tf_op | source)
XLA Modules:
  0.0 108.4 jit_solution(17467198474466862822)
XLA Ops:
  0.6 104.6 %swiglu_panel.1 = (bf16[256,256]{1,0:T(8,128)(2,1)}, bf16[512,256]{1,0:T(8,128)(2,1)}) custom-call(f32[1,16384]{1,0:T(1,128)} %bitcast.2, s32[4]{0:T(128)} %owner.1, s32[4]{0:T(128)} %lengths.1, s32[1,512]{1,0:T(1,128)} %bitcast.3, bf16[512,4096]{1,0:T(8,128)(2,1)} %tok_hbm.1, bf16[256,256]{1,0:T(8,128)(2,1)} %gate_w.1, bf16[256,256]{1,0:T(8,128)(2,1)} %up_w.1), custom_call_target="tpu_custom_call" | custom-call | tf_op jit(solution)/shard_map/swiglu_panel/pallas_call | solution.py:498
  105.2 1.6 %copy.11 = bf16[256,256]{1,0:T(8,128)(2,1)} copy(bf16[256,256]{1,0:T(8,128)(2,1)} %get-tuple-element.4) | data formatting | bytes 262144
  106.8 1.7 %copy.12 = bf16[512,256]{1,0:T(8,128)(2,1)} copy(bf16[512,256]{1,0:T(8,128)(2,1)} %get-tuple-element.5) | data formatting | bytes 524288

commit v4 on v3

--- a/solution.py
+++ b/solution.py
@@ -19,6 +19,9 @@
 TOK = 512
 ROWS = 256
 HID = 256
+GROUPS = 2
+PART = ROWS // GROUPS
+PEERS = N_REQ // GROUPS
 FEAT = 4096
 PAIR = 4
 NQ = 4
@@ -124,7 +127,7 @@
     earlier = lax.broadcasted_iota(jnp.int32, (TOK, TOK), 0) < lax.broadcasted_iota(jnp.int32, (TOK, TOK), 1)
     before = jnp.dot(marks.astype(bf16), earlier.astype(f32).astype(bf16), preferred_element_type=f32)
     rank = jnp.sum(before * marks, axis=0, keepdims=True)
-    row = jnp.where(live, rank * N_REQ + to.astype(f32), -1.0)
+    row = jnp.where(live, rank * PEERS + (to // PEERS * PART + to % PEERS).astype(f32), -1.0)
     pick[...] = (lax.broadcasted_iota(jnp.int32, (ROWS, TOK), 0).astype(f32) == row).astype(f32).astype(bf16)
     fetch.wait()
 
@@ -331,42 +334,50 @@
         y_arrived(q, zz, 1 - zz, ra, s_ring_in.at[q, zz, 1 - zz], zz)
         y_arrived(q, zz, 2, ra, s_ring_in.at[q, zz, 2], zz)
 
-    keep = pl.ds(pl.multiple_of(c * ROWS, ROWS), ROWS)
-    pass_on = pl.ds(pl.multiple_of((1 - c) * ROWS, ROWS), ROWS)
-
-    def part_copy(q, k):
+    def part_copy(q, k, g):
+        here, there = pl.ds(pl.multiple_of((1 - c) * ROWS + g * PART, PART), PART), pl.ds(g * PART, PART)
         return remote(
-            part.at[q, k, pass_on], part_in.at[q, k], s_part_out.at[q, k], s_part_in.at[q, k], (req, 2 * j + 1 - c)
+            part.at[q, k, here], part_in.at[q, k, there],
+            s_part_out.at[q, k, g], s_part_in.at[q, k, g], (req, 2 * j + 1 - c),
         )
 
     def dot(q):
         for k in range(2):
             w = panel[q, :, :, :, k * HID : (k + 1) * HID].reshape(8 * ROWS, HID)
             part[q, k] = jnp.dot(act[...], w, preferred_element_type=f32)
-            part_copy(q, k).start()
-
-    def red_copy(q, k):
+            for g in range(GROUPS):
+                part_copy(q, k, g).start()
+
+    def red_copy(q, k, g):
         device = at(2 * c + lax.rem(q, 2), y, z, k)
-        return remote(red_out.at[q, k], red_in.at[x, q // 2], s_red_out.at[q, k], s_red_in.at[x, q // 2], device)
+        rows = pl.ds(g * PART, PART)
+        return remote(
+            red_out.at[q, k, rows], red_in.at[x, q // 2, rows],
+            s_red_out.at[q, k, g], s_red_in.at[x, q // 2, g], device,
+        )
 
     def red_here(q, k):
         return jnp.logical_and(2 * c + lax.rem(q, 2) == x, c == k)
 
     def total(q):
-        for k in range(2):
-            arrived(part_in.at[q, k], s_part_in.at[q, k])
-            both = (part[q, k, keep] + part_in[q, k]).astype(bf16)
-            here = red_here(q, k)
-
-            @pl.when(here)
-            def _():
-                red_in[x, q // 2] = both
-
-            @pl.when(jnp.logical_not(here))
-            def _():
-                red_out[q, k] = both
-                red_copy(q, k).start()
-
+        for g in range(GROUPS):
+            rows = pl.ds(g * PART, PART)
+            mine_g = pl.ds(pl.multiple_of(c * ROWS + g * PART, PART), PART)
+            for k in range(2):
+                arrived(part_in.at[q, k, rows], s_part_in.at[q, k, g])
+                both = (part[q, k, mine_g] + part_in[q, k, rows]).astype(bf16)
+                here = red_here(q, k)
+
+                @pl.when(here)
+                def _():
+                    red_in[x, q // 2, rows] = both
+
+                @pl.when(jnp.logical_not(here))
+                def _():
+                    red_out[q, k, rows] = both
+                    red_copy(q, k, g).start()
+
+    def left(q):
         for zz in range(2):
             d, up, down = reach(q, zz)
             for way, on in enumerate((up, down)):
@@ -384,7 +395,8 @@
                 edge_copy(q, k).wait_send()
 
         for k in range(2):
-            part_copy(q, k).wait_send()
+            for g in range(GROUPS):
+                part_copy(q, k, g).wait_send()
 
     first = (hops(1) < hops(0)).astype(jnp.int32)
 
@@ -427,39 +439,48 @@
 
         each_chunk(t, DOT_T, dot)
         each_chunk(t, TOTAL_T, total)
+        each_chunk(t, TOTAL_T[:-1], left)
         return 0
 
     lax.fori_loop(0, TOTAL_T[-1] + 1, turn, 0)
 
-    for k in range(NX):
-        @pl.when(jnp.logical_or(x != k, h != c))
-        def _():
-            for kind in range(2):
-                arrived(red_in.at[k, kind], s_red_in.at[k, kind])
-
-    def joined(kind):
-        both = red_in[0, kind].astype(f32)
-        for k in range(1, NX):
-            both = both + red_in[k, kind].astype(f32)
-        return both
-
-    gate = joined(0)
-    hid[...] = (gate / (1.0 + jnp.exp(-gate)) * joined(1)).astype(bf16)
-
-    for half in range(2):
-        wide[...] = hid[:, half * 128 : (half + 1) * 128].astype(f32)
-        for k in range(PAIR):
-            a2a_out[pl.ds(half * PAIR + k, N_REQ, stride=8), :] = wide[k * N_REQ : (k + 1) * N_REQ, :]
-
     my_tile = pl.ds(pl.multiple_of(req * 8, 8), 8)
 
-    def send_tile(i, _):
-        to_req = lax.rem(req + i, N_REQ)
+    def send_tile(to_req):
         src = a2a_out.at[pl.ds(pl.multiple_of(to_req * 8, 8), 8)]
         remote(src, a2a_in.at[my_tile], s_a2a_out, s_a2a_in, (to_req, own)).start()
-        return 0
-
-    lax.fori_loop(1, N_REQ, send_tile, 0)
+
+    for g in range(GROUPS):
+        rows = pl.ds(g * PART, PART)
+        for k in range(NX):
+            @pl.when(jnp.logical_or(x != k, h != c))
+            def _():
+                for kind in range(2):
+                    arrived(red_in.at[k, kind, rows], s_red_in.at[k, kind, g])
+
+        gate, up = red_in[0, 0, rows].astype(f32), red_in[0, 1, rows].astype(f32)
+        for k in range(1, NX):
+            gate = gate + red_in[k, 0, rows].astype(f32)
+            up = up + red_in[k, 1, rows].astype(f32)
+        hidden = (gate / (1.0 + jnp.exp(-gate)) * up).astype(bf16)
+        hid[rows] = hidden
+        hidden = hidden.astype(f32)
+        for half in range(2):
+            for k in range(PAIR):
+                a2a_out[pl.ds(g * 8 * PEERS + half * PAIR + k, PEERS, stride=8), :] = hidden[
+                    k * PEERS : (k + 1) * PEERS, half * 128 : (half + 1) * 128
+                ]
+
+        def send_near(i, _):
+            send_tile(PEERS * g + lax.rem(req + i, PEERS))
+            return 0
+
+        lax.fori_loop(1, PEERS, send_near, 0)
+
+        @pl.when(req // PEERS != g)
+        def _():
+            send_tile(PEERS * g + lax.rem(req, PEERS))
+
     local_out[...] = lax.dot_general(
         pick[...], hid[...], (((0,), (0,)), ((), ())), preferred_element_type=f32
     ).astype(bf16)
@@ -467,11 +488,13 @@
     keep_local.start()
     a2a_in[my_tile, :] = a2a_out[my_tile, :]
 
+    left(NQ - 1)
     for q in range(NQ):
         for k in range(2):
             @pl.when(jnp.logical_not(red_here(q, k)))
             def _():
-                red_copy(q, k).wait_send()
+                for g in range(GROUPS):
+                    red_copy(q, k, g).wait_send()
     give.wait_send()
     for cp in sq_sends:
         cp.wait_send()
@@ -522,7 +545,7 @@
             dma, dma((2,)), dma((2,)), dma((N_OWN,)), dma((N_OWN,)), dma((7,)), dma((8,)),
             dma((NQ, 2, 2)), dma((NQ, 2)), dma((NQ, 2, 3)), dma((NQ, 2, 3)), dma((NQ, 3)), dma((NQ, 3)),
             dma((NQ, 2, NY, 2)), dma((NQ, 2, NY)),
-            dma((NQ, 2)), dma((NQ, 2)), dma((NQ, 2)), dma((NX, 2)), dma, dma, dma,
+            dma((NQ, 2, GROUPS)), dma((NQ, 2, GROUPS)), dma((NQ, 2, GROUPS)), dma((NX, 2, GROUPS)), dma, dma, dma,
             pltpu.SemaphoreType.REGULAR((6,)),
         ],
         compiler_params=pltpu.CompilerParams(

time: 110 us -> 108 us (0.982)
  the two profiles are of different devices: /device:TPU:3 before, /device:TPU:5 now
where the time goes in v4:
time: 108 us
  Pallas kernels  104 us (96%)
  local copies, waits for them, and re-layouts  3.24 us (3%)
    pallas_call x1, Pallas kernels, body(): pl.pallas_call(kernel, out_shape=(jax.ShapeDtypeStruct((ROWS, HID), bf16)...  104 us
    unnamed x2, local copies, waits for them, and re-layouts  3.24 us

profile of v4, /device:TPU:5, one launch (start us, length us, event | category | flops | bytes accessed | tf_op | source)
XLA Modules:
  0.0 108.2 jit_solution(9552505362825822124)
XLA Ops:
  0.6 104.3 %swiglu_panel.1 = (bf16[256,256]{1,0:T(8,128)(2,1)}, bf16[512,256]{1,0:T(8,128)(2,1)}) custom-call(f32[1,16384]{1,0:T(1,128)} %bitcast.2, s32[4]{0:T(128)} %owner.1, s32[4]{0:T(128)} %lengths.1, s32[1,512]{1,0:T(1,128)} %bitcast.3, bf16[512,4096]{1,0:T(8,128)(2,1)} %tok_hbm.1, bf16[256,256]{1,0:T(8,128)(2,1)} %gate_w.1, bf16[256,256]{1,0:T(8,128)(2,1)} %up_w.1), custom_call_target="tpu_custom_call" | custom-call | tf_op jit(solution)/shard_map/swiglu_panel/pallas_call | solution.py:521
  105.0 1.6 %copy.11 = bf16[256,256]{1,0:T(8,128)(2,1)} copy(bf16[256,256]{1,0:T(8,128)(2,1)} %get-tuple-element.4) | data formatting | bytes 262144
  106.6 1.7 %copy.12 = bf16[512,256]{1,0:T(8,128)(2,1)} copy(bf16[512,256]{1,0:T(8,128)(2,1)} %get-tuple-element.5) | data formatting | bytes 524288

commit v5 on v4

--- a/solution.py
+++ b/solution.py
@@ -47,7 +47,7 @@
     gain, owner, lengths, dest, tok_hbm, gate_w, up_w,
     packed_out, local_hbm,
     tok, pick, act, act_out, panel, root_up, squares, squares_out, squares_in,
-    part, part_in, red_out, red_in, hid, local_out, a2a_out, a2a_in, wide,
+    part, part_out, part_in, red_out, red_in, hid, local_out, a2a_out, a2a_in, wide,
     s_tok, s_act, s_root_out, s_gate_in, s_up_in, s_sq_out, s_sq_in,
     s_chain_out, s_chain_in, s_ring_out, s_ring_in, s_edge_out, s_edge_in, s_spread_out, s_spread_in,
     s_part_out, s_part_in, s_red_out, s_red_in, s_a2a_out, s_a2a_in, s_local, relay,
@@ -335,9 +335,9 @@
         y_arrived(q, zz, 2, ra, s_ring_in.at[q, zz, 2], zz)
 
     def part_copy(q, k, g):
-        here, there = pl.ds(pl.multiple_of((1 - c) * ROWS + g * PART, PART), PART), pl.ds(g * PART, PART)
+        rows = pl.ds(g * PART, PART)
         return remote(
-            part.at[q, k, here], part_in.at[q, k, there],
+            part_out.at[q, k, rows], part_in.at[q, k, rows],
             s_part_out.at[q, k, g], s_part_in.at[q, k, g], (req, 2 * j + 1 - c),
         )
 
@@ -345,6 +345,8 @@
         for k in range(2):
             w = panel[q, :, :, :, k * HID : (k + 1) * HID].reshape(8 * ROWS, HID)
             part[q, k] = jnp.dot(act[...], w, preferred_element_type=f32)
+            there = pl.ds(pl.multiple_of((1 - c) * ROWS, ROWS), ROWS)
+            part_out[q, k] = part[q, k, there].astype(bf16)
             for g in range(GROUPS):
                 part_copy(q, k, g).start()
 
@@ -365,7 +367,7 @@
             mine_g = pl.ds(pl.multiple_of(c * ROWS + g * PART, PART), PART)
             for k in range(2):
                 arrived(part_in.at[q, k, rows], s_part_in.at[q, k, g])
-                both = (part[q, k, mine_g] + part_in[q, k, rows]).astype(bf16)
+                both = (part[q, k, mine_g] + part_in[q, k, rows].astype(f32)).astype(bf16)
                 here = red_here(q, k)
 
                 @pl.when(here)
@@ -534,7 +536,8 @@
             pltpu.VMEM((8, ROWS), f32),
             pltpu.VMEM((8, 8, ROWS), f32),
             pltpu.VMEM((NQ, 2, 2 * ROWS, HID), f32),
-            pltpu.VMEM((NQ, 2, ROWS, HID), f32),
+            pltpu.VMEM((NQ, 2, ROWS, HID), bf16),
+            pltpu.VMEM((NQ, 2, ROWS, HID), bf16),
             pltpu.VMEM((NQ, 2, ROWS, HID), bf16),
             pltpu.VMEM((NX, 2, ROWS, HID), bf16),
             pltpu.VMEM((ROWS, HID), bf16),

time: 108 us -> 109 us (level)
  the two profiles are of different devices: /device:TPU:5 before, /device:TPU:37 now
where the time goes in v5:
time: 109 us
  Pallas kernels  105 us (96%)
  local copies, waits for them, and re-layouts  3.24 us (3%)
    pallas_call x1, Pallas kernels, body(): pl.pallas_call(kernel, out_shape=(jax.ShapeDtypeStruct((ROWS, HID), bf16)...  105 us
    unnamed x2, local copies, waits for them, and re-layouts  3.24 us

profile of v5, /device:TPU:37, one launch (start us, length us, event | category | flops | bytes accessed | tf_op | source)
XLA Modules:
  0.0 109.1 jit_solution(3999313742903526784)
XLA Ops:
  0.6 105.2 %swiglu_panel.1 = (bf16[256,256]{1,0:T(8,128)(2,1)}, bf16[512,256]{1,0:T(8,128)(2,1)}) custom-call(f32[1,16384]{1,0:T(1,128)} %bitcast.2, s32[4]{0:T(128)} %owner.1, s32[4]{0:T(128)} %lengths.1, s32[1,512]{1,0:T(1,128)} %bitcast.3, bf16[512,4096]{1,0:T(8,128)(2,1)} %tok_hbm.1, bf16[256,256]{1,0:T(8,128)(2,1)} %gate_w.1, bf16[256,256]{1,0:T(8,128)(2,1)} %up_w.1), custom_call_target="tpu_custom_call" | custom-call | tf_op jit(solution)/shard_map/swiglu_panel/pallas_call | solution.py:523
  105.8 1.6 %copy.11 = bf16[256,256]{1,0:T(8,128)(2,1)} copy(bf16[256,256]{1,0:T(8,128)(2,1)} %get-tuple-element.4) | data formatting | bytes 262144
  107.4 1.7 %copy.12 = bf16[512,256]{1,0:T(8,128)(2,1)} copy(bf16[512,256]{1,0:T(8,128)(2,1)} %get-tuple-element.5) | data formatting | bytes 524288

commit v6 on v4

--- a/solution.py
+++ b/solution.py
@@ -31,7 +31,7 @@
 EDGE_T = (0, 4, 5, 9)
 ORDER = (0, 3, 1, 2)
 LAGS = (0, 4, 6, 10, 11)
-RING_ON, RING_END, JOIN, GIVE_T, RELAY_T = 4, 8, 2, 8, 2
+RING_ON, RING_END, JOIN, GIVE_T, RELAY_T = 4, 8, 2, 7, 2
 STREAM = 5 * NQ
 LOAD_T = tuple(min(a, b) for a, b in zip(CHAIN_T, EDGE_T))
 REST_T = [n for n in range(STREAM) if n not in CHAIN_T]
@@ -422,6 +422,7 @@
 
     def turn(t, _):
         once(t, near + GIVE_T, give.start)
+        once(t, near + GIVE_T - 2, normalize_mine)
         for i in range(1, 7):
             once(t, i * RELAY_T, pass_word, i)
 
@@ -434,7 +435,6 @@
 
         @pl.when(t == DOT_T[0] - 1)
         def _():
-            normalize_mine()
             normalize_given()
 
         each_chunk(t, DOT_T, dot)

time: 108 us -> 108 us (level)
  no operation moved by 1% of the time
where the time goes in v6:
time: 108 us
  Pallas kernels  104 us (96%)
  local copies, waits for them, and re-layouts  3.24 us (3%)
    pallas_call x1, Pallas kernels, body(): pl.pallas_call(kernel, out_shape=(jax.ShapeDtypeStruct((ROWS, HID), bf16)...  104 us
    unnamed x2, local copies, waits for them, and re-layouts  3.24 us

profile of v6, /device:TPU:5, one launch (start us, length us, event | category | flops | bytes accessed | tf_op | source)
XLA Modules:
  0.0 108.0 jit_solution(2273024221881456826)
XLA Ops:
  0.6 104.2 %swiglu_panel.1 = (bf16[256,256]{1,0:T(8,128)(2,1)}, bf16[512,256]{1,0:T(8,128)(2,1)}) custom-call(f32[1,16384]{1,0:T(1,128)} %bitcast.2, s32[4]{0:T(128)} %owner.1, s32[4]{0:T(128)} %lengths.1, s32[1,512]{1,0:T(1,128)} %bitcast.3, bf16[512,4096]{1,0:T(8,128)(2,1)} %tok_hbm.1, bf16[256,256]{1,0:T(8,128)(2,1)} %gate_w.1, bf16[256,256]{1,0:T(8,128)(2,1)} %up_w.1), custom_call_target="tpu_custom_call" | custom-call | tf_op jit(solution)/shard_map/swiglu_panel/pallas_call | solution.py:521
  104.8 1.6 %copy.11 = bf16[256,256]{1,0:T(8,128)(2,1)} copy(bf16[256,256]{1,0:T(8,128)(2,1)} %get-tuple-element.4) | data formatting | bytes 262144
  106.4 1.7 %copy.12 = bf16[512,256]{1,0:T(8,128)(2,1)} copy(bf16[512,256]{1,0:T(8,128)(2,1)} %get-tuple-element.5) | data formatting | bytes 524288
